TPU v7x, 32 devices: a whole 2x2x4 slice. The times are simulated.
32 devices in a mesh: col: 8 (over z, y), row: 4 (over x, core).
Axes of the slice: x: 2, y: 2, z: 4, core: 2. Of those that a mesh axis runs over, the one named last changes fastest.
Arguments:
- pivot_block: bfloat16 [512, 512], P(None, 'row'), may hold values from -0.5 to 5.5, as said below
- panel: bfloat16 [4, 256, 512], P('row', 'col'), may hold values from -1.1953125 to 1.1953125
- lead: int32 [4, 2], P('row'), may hold values from 0 to 3
- trailing: bfloat16 [1024, 1024], P('row', 'col'), may hold values from -1.796875 to 1.796875
Outputs:
- pivot_factor: float32 [512, 512], P(None, 'row')
- panel_factor: bfloat16 [4, 256, 512], P('row', 'col')
- schur: bfloat16 [1024, 1024], P('row', 'col')
Inputs may be any that keep to these rules, and one draw needn't show every extreme that they name: `pivot_block`: symmetric positive definite.
All inputs are finite; a program needn't handle non-finite values.
Results may differ from a plain program's by a relative error of at most 0.0042.
Values may be sent and summed in bfloat16 or wider, within the bound.
No kernel may reach another device: no remote copies, remote signals or barrier semaphores. Data moves between devices by JAX's collectives and lax.ppermute only.
A program may use at most 64 MiB of HBM per device.

v0:
```python
import functools

import jax
import jax.numpy as jnp
from jax import lax
from jax.experimental import pallas as pl
from jax.experimental.pallas import tpu as pltpu
from jax.sharding import PartitionSpec as P

BLOCK = 128
STRIP = 32
SUB = 16
GROUP = 8
LANES = 128


def split(value):
    high = value.astype(jnp.bfloat16)
    low = (value - high.astype(jnp.float32)).astype(jnp.bfloat16)
    return high, low


def row_of(value, row):
    return jnp.broadcast_to(value[row : row + 1, :], (GROUP, LANES))


def reciprocal(value):
    guess = pl.reciprocal(value, approx=True)
    return guess, 2.0 - value * guess


def eliminate_strip(strip, first):
    groups = STRIP // GROUP
    sublane = lax.broadcasted_iota(jnp.int32, (GROUP, LANES), 0)
    lane = lax.broadcasted_iota(jnp.int32, (GROUP, LANES), 1)
    zero = jnp.zeros((GROUP, LANES), jnp.float32)
    block = [strip[g * GROUP : (g + 1) * GROUP, :] for g in range(groups)]
    inside = (lane >= first) & (lane < first + STRIP)
    lower = [zero] * groups
    column = [None] * STRIP
    for k in range(0, STRIP, 2):
        if k % SUB == 0:
            for j in range(k, k + SUB):
                column[j] = [
                    jnp.broadcast_to(block[g][:, first + j : first + j + 1], (GROUP, LANES)) if g >= j // GROUP else None
                    for g in range(groups)
                ]
            taken = (lane >= first + k) & (lane < first + k + SUB)
            for g in range(groups):
                identity = jnp.where(lane - first == sublane + g * GROUP, 1.0, 0.0)
                block[g] = jnp.where(taken, identity, block[g])
        last = k - k % SUB + SUB
        home, sub = k // GROUP, k % GROUP
        u, v = column[k], column[k + 1]
        a = row_of(u[home], sub)
        b = row_of(u[home], sub + 1)
        c = row_of(v[home], sub + 1)
        det = a * c - b * b
        guess, correction = reciprocal(det)
        n1 = [None if g < home else c * u[g] - b * v[g] for g in range(groups)]
        n2 = [None if g < home else a * v[g] - b * u[g] for g in range(groups)]
        w1 = [None if g < home else (n1[g] * guess) * correction for g in range(groups)]
        w2 = [None if g < home else (n2[g] * guess) * correction for g in range(groups)]
        for j in range(k + 2, last):
            at, row = j // GROUP, j % GROUP
            uj, vj = row_of(u[at], row), row_of(v[at], row)
            for g in range(at, groups):
                if j < k + 4:
                    step = ((n1[g] * uj + n2[g] * vj) * guess) * correction
                else:
                    step = w1[g] * uj + w2[g] * vj
                column[j][g] = column[j][g] - step
        root_a = lax.rsqrt(a)
        root_d = lax.rsqrt(a * det)
        for g in range(home, groups):
            lower[g] = jnp.where(lane == first + k, u[g] * root_a, lower[g])
            lower[g] = jnp.where(lane == first + k + 1, n2[g] * root_d, lower[g])
        below = sublane > sub + 1
        w1[home] = jnp.where(below, w1[home], 0.0)
        w2[home] = jnp.where(below, w2[home], 0.0)
        t0, t1 = row_of(block[home], sub), row_of(block[home], sub + 1)
        for g in range(home, groups):
            block[g] = block[g] - (w1[g] * t0 + w2[g] * t1)
        block[home] = jnp.where(sublane == sub, t0 * root_a, block[home])
        block[home] = jnp.where(sublane == sub + 1, (a * t1 - b * t0) * root_d, block[home])
    for g in range(groups):
        keep = (lane <= first + sublane + g * GROUP) & inside
        lower[g] = jnp.where(keep, lower[g], 0.0)
    return jnp.concatenate(block, axis=0), jnp.concatenate(lower, axis=0)


def matmul(left, right):
    return jnp.dot(left, right, preferred_element_type=jnp.float32)


def stacked(value):
    high, low = split(value)
    return jnp.concatenate([high, high, low, jnp.zeros_like(high)], axis=0)


def rows_at(block):
    return pl.ds(pl.multiple_of(block * LANES, LANES), LANES)


def square_iota(axis):
    return lax.broadcasted_iota(jnp.int32, (LANES, LANES), axis)


def beyond_strip():
    return square_iota(1) // STRIP > square_iota(0) // STRIP


def eliminate_block(rows, lower_ref):
    lane = square_iota(1)
    done = [[] for _ in rows]
    for first in range(0, LANES, STRIP):
        last = first + STRIP
        solved, diagonal = eliminate_strip(rows[0][:STRIP], first)
        lower_ref[first:last, :] = diagonal
        in_strip = (lane[:STRIP] >= first) & (lane[:STRIP] < last)
        high, low = split(jnp.where(in_strip, solved, 0.0))
        high, low = high.astype(jnp.float32), low.astype(jnp.float32)
        inverse = high if first == 0 else pltpu.roll(high, LANES - first, 1)
        inverse += pltpu.roll(low, (LANES + STRIP - first) % LANES, 1) if first != STRIP else low
        inverse += pltpu.roll(high, (LANES + 2 * STRIP - first) % LANES, 1) if first != 2 * STRIP else high
        inverse = inverse.astype(jnp.bfloat16)
        strips = [solved] + [matmul(inverse, stacked(part[:STRIP])) for part in rows[1:]]
        for part, strip in zip(done, strips):
            part.append(strip)
        if last == LANES:
            break
        high, low = split(solved)
        wide = jnp.concatenate([high, low, high, jnp.zeros_like(high)], axis=0).astype(jnp.float32)
        left = wide.T[last:, :].astype(jnp.bfloat16)
        under = [part[STRIP:] for part in rows]
        inside = (lane[last:] >= first) & (lane[last:] < last)
        under[0] = jnp.where(inside, 0.0, under[0])
        rows = [part - matmul(left, stacked(strip)) for part, strip in zip(under, strips)]
    return [jnp.concatenate(part, axis=0) for part in done]


def assemble(me, own, mate, far, far_mate, work):
    size = own.shape[0]
    half = size // 2
    near = ((own, me), (mate, jnp.bitwise_xor(me, 1)))
    other = ((far, jnp.bitwise_xor(me, 2)), (far_mate, jnp.bitwise_xor(me, 3)))

    @pl.when(me < 2)
    def _():
        for part, column in near:
            work[column, :half, :] = part[:half, :].astype(jnp.float32)
            for block in range(half // LANES, size // LANES):
                flipped = part[block * LANES : (block + 1) * LANES, :].astype(jnp.float32).T
                work[block, rows_at(column), :] = flipped
        for part, column in other:
            work[column, half:size, :] = part[...].astype(jnp.float32)

    @pl.when(me >= 2)
    def _():
        for part, column in near:
            work[column, :size, :] = part[...].astype(jnp.float32)
        for part, column in other:
            work[column, :half, :] = part[...].astype(jnp.float32)


def first_kernel(axis, own, mate, far, far_mate, done_ref, lower_ref, work):
    count = lax.axis_size(axis)
    assemble(lax.axis_index(axis), own, mate, far, far_mate, work)
    done = eliminate_block([work[d, :LANES, :] for d in range(count)], lower_ref)
    for d in range(count):
        done_ref[d] = done[d]


def rest_kernel(
    axis, own, mate, far, far_mate, done_ref, first_lower, own_ref, high_ref, low_ref, work, lower
):
    count = lax.axis_size(axis)
    me = lax.axis_index(axis)
    lane, row = square_iota(1), square_iota(0)
    beyond = beyond_strip()
    assemble(me, own, mate, far, far_mate, work)
    work[:count, :LANES, :] = done_ref[...]
    lower[0] = first_lower[...]

    def block_step(q, carry):
        before = q - 1
        places = [lax.rem(before + d, count) for d in range(count)]
        rights = [work[place, rows_at(before), :] for place in places]
        rights[0] = jnp.where(beyond, 0.0, rights[0])
        rights = [split(right) for right in rights]

        def update(target):
            high, low = split(work[target, rows_at(before), :].T)
            both = jnp.concatenate([high, low], axis=1)
            new = []
            for d, (place, (right_high, right_low)) in enumerate(zip(places, rights)):
                product = matmul(both, jnp.concatenate([right_high, right_high], axis=0)) + matmul(high, right_low)
                new.append(-product if d == 0 else work[place, rows_at(target), :] - product)
            return new

        rows = update(q)
        for target in (q + 1, q + 2):
            for place, new in zip(places, update(target)):
                work[place, rows_at(target), :] = new
        done = eliminate_block(rows[1:] + rows[:1], lower.at[q])
        for place, part in zip(places[1:] + places[:1], done):
            work[place, rows_at(q), :] = part
        return carry

    lax.fori_loop(1, count, block_step, 0)

    for i in range(count):
        block = work[i, rows_at(me), :]
        upper = jnp.where((i > me) | ((i == me) & beyond), block, 0.0)
        own_ref[i * LANES : (i + 1) * LANES, :] = upper.T + jnp.where(i == me, lower[i], 0.0)
        for c in range(count):
            block = work[c, i * LANES : (i + 1) * LANES, :]
            if c > i:
                block = jnp.zeros_like(block)
            elif c == i:
                block = jnp.where(lane <= row, block, 0.0)
            high, low = split(block)
            high_ref[i * LANES : (i + 1) * LANES, c * LANES : (c + 1) * LANES] = high
            low_ref[i * LANES : (i + 1) * LANES, c * LANES : (c + 1) * LANES] = low


def solve_kernel(row_axis, col_axis, order, group_count, *refs):
    high_ref, low_ref = refs[:2]
    inputs = refs[2 : 3 + group_count]
    trailing_ref, own_ref, schur_ref, group, side = refs[3 + group_count :]
    size = high_ref.shape[0]
    half = size // 2
    share = own_ref.shape[1]
    count = side.shape[0] // share
    my_row, my_col = lax.axis_index(row_axis), lax.axis_index(col_axis)
    for i, ref in enumerate(inputs[:-1]):
        if order is None:
            group[...] = ref[...]
        else:
            for p in range(count):
                at = jnp.bitwise_xor(my_col, i * count + p) * share
                group[pl.ds(pl.multiple_of(at, share), share), :] = ref[p * share : (p + 1) * share, :]
    for p in range(count):
        place = jnp.bitwise_xor(my_row, p) if order else lax.rem(my_row + count - p, count)
        side[pl.ds(pl.multiple_of(place * share, share), share), :] = inputs[-1][p * share : (p + 1) * share, :]
    contract = (((1,), (1,)), ((), ()))

    def product(left, right):
        return lax.dot_general(left, right, contract, preferred_element_type=jnp.float32)

    def solve(rows):
        first = product(rows[:, :half], high_ref[:half, :half]) + product(rows[:, :half], low_ref[:half, :half])
        second = product(rows, high_ref[half:, :]) + product(rows, low_ref[half:, :])
        return jnp.concatenate([first, second], axis=1).astype(jnp.bfloat16)

    side[...] = solve(side[...])
    rows = group.shape[0]
    chunk = min(rows, 256)

    def step(i, carry):
        here = pl.ds(pl.multiple_of(i * chunk, chunk), chunk)
        solved = solve(group[here, :])
        group[here, :] = solved
        update = product(solved, side[...])
        schur_ref[here, :] = (trailing_ref[here, :].astype(jnp.float32) - update).astype(jnp.bfloat16)
        return carry

    if rows == chunk:
        step(0, 0)
    else:
        lax.fori_loop(0, rows // chunk, step, 0)
    own_ref[0] = group[pl.ds(pl.multiple_of(my_col * share, share), share), :]


def body(pivot_block, panel, lead, trailing):
    pivot_size, local_width = pivot_block.shape
    rows, cols = lax.axis_size("row"), lax.axis_size("col")
    share = panel.shape[1]
    col_index = lax.axis_index("col")
    vmem = pl.BlockSpec(memory_space=pltpu.VMEM)

    half = pivot_size // 2
    row_index = lax.axis_index("row")
    wide = pivot_block.astype(jnp.float32)
    diagonal_half = lax.dynamic_slice_in_dim(pivot_block, row_index // 2 * half, half, 0)
    far = lax.ppermute(diagonal_half, "row", [(d ^ 2, d) for d in range(rows)])
    far_mate = lax.ppermute(diagonal_half, "row", [(d ^ 3, d) for d in range(rows)])
    mate = lax.ppermute(pivot_block, "row", [(d ^ 1, d) for d in range(rows)])
    pivots = [wide, mate, far, far_mate]

    done, first_lower = pl.pallas_call(
        functools.partial(first_kernel, "row"),
        out_shape=(
            jax.ShapeDtypeStruct((rows, LANES, LANES), jnp.float32),
            jax.ShapeDtypeStruct((LANES, LANES), jnp.float32),
        ),
        in_specs=[vmem] * len(pivots),
        out_specs=(vmem,) * 2,
        scratch_shapes=[pltpu.VMEM((rows, pivot_size, LANES), jnp.float32)],
        compiler_params=pltpu.CompilerParams(vmem_limit_bytes=32 * 1024 * 1024),
        cost_estimate=pl.CostEstimate(flops=3 * 10**8, bytes_accessed=10**6, transcendentals=10**5),
        name="first",
    )(*pivots)

    def live(shards, rows_of):
        block = jnp.concatenate([(shard * share + jnp.arange(share)) // BLOCK for shard in shards])
        matches = block[:, None] == jnp.arange(lead.shape[1])[None, :]
        row_lead = jnp.sum(jnp.where(matches, lead, 0), axis=1)
        keep = (jnp.arange(pivot_size) // BLOCK)[None, :] >= row_lead[:, None]
        return jnp.where(keep, rows_of, jnp.zeros_like(rows_of))

    ratio = cols // rows
    paired = cols == 2 * rows and rows & (rows - 1) == 0

    def to_side(array, shift):
        pairs = []
        for r in range(rows):
            for c in range(cols):
                to_row, to_col = (c % rows + shift) % rows, r * ratio + c // rows
                pairs.append((c * rows + r, to_col * rows + to_row))
        return lax.ppermute(array, ("col", "row"), pairs)

    if paired:
        quad, _ = lax.optimization_barrier((panel[0], diagonal_half))
        step = 1
        while step < rows:
            pieces = (quad, lax.ppermute(quad, "col", [(d ^ step, d) for d in range(cols)]))
            step *= 2
            if step == rows:
                pieces, _ = lax.optimization_barrier((pieces, first_lower))
            quad = jnp.concatenate(pieces, axis=0)
        quad = live([col_index ^ p for p in range(rows)], quad)
        group = [quad, lax.ppermute(quad, "col", [(d ^ rows, d) for d in range(cols)])]
        side = to_side(quad, 0)
    else:
        masked = live([col_index], panel[0])
        group = [lax.all_gather(masked, "col", axis=0, tiled=True)]
        side = jnp.concatenate([to_side(masked, s) for s in range(rows)], axis=0)

    own, high, low = pl.pallas_call(
        functools.partial(rest_kernel, "row"),
        out_shape=(
            jax.ShapeDtypeStruct((pivot_size, local_width), jnp.float32),
            jax.ShapeDtypeStruct((pivot_size, pivot_size), jnp.bfloat16),
            jax.ShapeDtypeStruct((pivot_size, pivot_size), jnp.bfloat16),
        ),
        in_specs=[vmem] * (len(pivots) + 2),
        out_specs=(vmem,) * 3,
        scratch_shapes=[
            pltpu.VMEM((rows + 2, pivot_size + 2 * LANES, LANES), jnp.float32),
            pltpu.VMEM((rows, LANES, LANES), jnp.float32),
        ],
        compiler_params=pltpu.CompilerParams(vmem_limit_bytes=32 * 1024 * 1024),
        cost_estimate=pl.CostEstimate(flops=10**9, bytes_accessed=2 * 10**6, transcendentals=10**5),
        name="rest",
    )(*pivots, done, first_lower)

    group_rows = share * cols
    panel_factor, schur = pl.pallas_call(
        functools.partial(solve_kernel, "row", "col", True if paired else None, len(group)),
        out_shape=(
            jax.ShapeDtypeStruct(panel.shape, jnp.bfloat16),
            jax.ShapeDtypeStruct(trailing.shape, jnp.bfloat16),
        ),
        in_specs=[vmem] * (4 + len(group)),
        out_specs=(vmem,) * 2,
        scratch_shapes=[
            pltpu.VMEM((group_rows, pivot_size), jnp.bfloat16),
            pltpu.VMEM((share * rows, pivot_size), jnp.bfloat16),
        ],
        compiler_params=pltpu.CompilerParams(vmem_limit_bytes=48 * 1024 * 1024),
        cost_estimate=pl.CostEstimate(flops=4 * 10**8, bytes_accessed=2 * 10**6, transcendentals=0),
        name="solve",
    )(high, low, *group, side, trailing)
    return (own, panel_factor, schur)


def solution(mesh):
    return jax.shard_map(
        body,
        mesh=mesh,
        in_specs=(P(None, "row"), P("row", "col", None), P("row", None), P("row", "col")),
        out_specs=(P(None, "row"), P("row", "col", None), P("row", "col")),
        check_vma=False,
    )
```

profile of v0, /device:TPU:1, one launch (start us, length us, event | category | flops | bytes accessed | tf_op | source)
XLA Modules:
  0.0 32.4 jit_solution(17527306208423851000)
XLA Ops:
  0.6 0.1 collective-permute-start
  0.8 0.9 %constant_dynamic-slice_fusion = bf16[256,128]{1,0:T(8,128)(2,1)S(1)} fusion(bf16[512,128]{1,0:T(8,128)(2,1)} %param.4, s32[]{:T(128)S(6)} %select_n.40), kind=kLoop, calls=%fused_computation.29 | loop fusion | bytes 131076 | tf_op jit(solution)/shard_map/dynamic_slice | solution.py:285
  1.7 2.7 %collective-permute-start.1 = (bf16[256,128]{1,0:T(8,128)(2,1)S(1)}, bf16[256,128]{1,0:T(8,128)(2,1)S(1)}, u32[]{:S(2)}, u32[]{:S(2)}) collective-permute-start(bf16[256,128]{1,0:T(8,128)(2,1)S(1)} %constant_dynamic-slice_fusion), channel_id=1, source_target_pairs={{2,0},{3,1},{0,2},{1,3},{6,4},{7,5},{4,6},{5,7},{10,8},{11,9},{8,1... | collective-permute-start | bytes 196616 | tf_op jit(solution)/shard_map/ppermute | solution.py:286
  4.3 0.0 collective-permute-start.2
  4.3 1.7 %collective-permute-start.3 = (bf16[32,512]{1,0:T(8,128)(2,1)S(1)}, bf16[32,512]{1,0:T(8,128)(2,1)S(1)}, u32[]{:S(2)}, u32[]{:S(2)}) collective-permute-start(bf16[32,512]{1,0:T(8,128)(2,1)S(1)} %bitcast.2), channel_id=1, source_target_pairs={{4,0},{0,4},{12,8},{8,12},{20,16},{16,20},{28,24},{24,28},{5,1},{1... | collective-permute-start | bytes 98312 | tf_op jit(solution)/shard_map/ppermute | solution.py:327
  6.1 0.1 pad_add_fusion
  6.1 0.7 %copy-done.3 = s32[1,2]{1,0:T(1,128)S(1)} copy-done((s32[1,2]{1,0:T(1,128)S(1)}, s32[1,2]{1,0:T(1,128)}, u32[]{:S(2)}) %copy-start.3) | copy-done | bytes 32
  6.8 0.1 fusion.3
  6.9 0.7 %collective-permute-done.3 = bf16[32,512]{1,0:T(8,128)(2,1)S(1)} collective-permute-done((bf16[32,512]{1,0:T(8,128)(2,1)S(1)}, bf16[32,512]{1,0:T(8,128)(2,1)S(1)}, u32[]{:S(2)}, u32[]{:S(2)}) %collective-permute-start.3) | collective-permute-done | bytes 32800 | tf_op jit(solution)/shard_map/ppermute | solution.py:327
  7.6 1.5 %collective-permute-start.4 = (bf16[64,512]{1,0:T(8,128)(2,1)S(1)}, bf16[64,512]{1,0:T(8,128)(2,1)S(1)}, u32[]{:S(2)}, u32[]{:S(2)}) collective-permute-start(bf16[64,512]{1,0:T(8,128)(2,1)S(1)} %constant_dynamic-update-slice_fusion), channel_id=1, source_target_pairs={{8,0},{12,4},{0,8},{4,12},{24,16},{28,20},{16,24},{20,28},{9,1},{1... | collective-permute-start | bytes 196616 | tf_op jit(solution)/shard_map/ppermute | solution.py:327
  9.2 0.0 copy-done.1
  9.2 0.0 collective-permute-done.1.far
  9.2 0.0 collective-permute-done.2.far_mate
  9.2 0.0 collective-permute-done.mate
  9.2 3.4 %first.1 = (f32[4,128,128]{2,1,0:T(8,128)S(1)}, f32[128,128]{1,0:T(8,128)S(1)}) custom-call(f32[512,128]{1,0:T(8,128)S(1)} %convert_element_type.3.own, bf16[512,128]{1,0:T(8,128)(2,1)S(1)} %collective-permute-done.mate, bf16[256,128]{1,0:T(8,128)(2,1)S(1)} %collective-permute-done.1.far, bf16[256,128]{1,0:T(8,128)(2,1)S(1)} %collective-permute-done.2.far_mate), custom_call_target="tpu_custom_call" | custom-call | flops 300000000 | bytes 1000000 | tf_op jit(solution)/shard_map/first/pallas_call | solution.py:291
  12.6 0.0 collective-permute-done.4
  12.6 0.1 compare_select_fusion.refs_2_
  12.7 2.4 %collective-permute-start.5 = (bf16[128,512]{1,0:T(8,128)(2,1)S(1)}, bf16[128,512]{1,0:T(8,128)(2,1)S(1)}, u32[]{:S(2)}, u32[]{:S(2)}) collective-permute-start(bf16[128,512]{1,0:T(8,128)(2,1)S(1)} %compare_select_fusion.refs_2_), channel_id=1, source_target_pairs={{16,0},{20,4},{24,8},{28,12},{0,16},{4,20},{8,24},{12,28},{17,1},{... | collective-permute-start | bytes 393224 | tf_op jit(solution)/shard_map/ppermute | solution.py:333
  15.1 3.9 %collective-permute-start.6 = (bf16[128,512]{1,0:T(8,128)(2,1)S(1)}, bf16[128,512]{1,0:T(8,128)(2,1)S(1)}, u32[]{:S(2)}, u32[]{:S(2)}) collective-permute-start(bf16[128,512]{1,0:T(8,128)(2,1)S(1)} %compare_select_fusion.refs_2_), channel_id=1, source_target_pairs={{0,0},{4,1},{8,2},{12,3},{16,4},{20,5},{24,6},{28,7},{1,8},{5,9},{... | collective-permute-start | bytes 393224 | tf_op jit(solution)/shard_map/ppermute | solution.py:321
  19.0 0.0 copy-start
  19.0 11.9 %rest.1 = (f32[512,128]{1,0:T(8,128)}, bf16[512,512]{1,0:T(8,128)(2,1)S(1)}, bf16[512,512]{1,0:T(8,128)(2,1)S(1)}) custom-call(f32[512,128]{1,0:T(8,128)S(1)} %convert_element_type.3.own, bf16[512,128]{1,0:T(8,128)(2,1)S(1)} %collective-permute-done.mate, bf16[256,128]{1,0:T(8,128)(2,1)S(1)} %collective-permute-done.1.far, ...), custom_call_target="tpu_custom_call" | custom-call | flops 1000000000 | bytes 2000000 | tf_op jit(solution)/shard_map/rest/pallas_call | solution.py:340
  30.9 0.0 collective-permute-done.5.refs_3_
  30.9 0.0 collective-permute-done.6.refs_4_
  30.9 1.5 %solve.1 = (bf16[1,32,512]{2,1,0:T(8,128)(2,1)}, bf16[256,128]{1,0:T(8,128)(2,1)}) custom-call(bf16[512,512]{1,0:T(8,128)(2,1)S(1)} %get-tuple-element.16.refs_0_, bf16[512,512]{1,0:T(8,128)(2,1)S(1)} %get-tuple-element.17.refs_1_, bf16[128,512]{1,0:T(8,128)(2,1)S(1)} %compare_select_fusion.refs_2_, bf16[128,512]{1,0:T(8,128)(2,1)S(1)} %collective-permute-done.5.refs_3_, ...), custom_call_target="tpu_custom_call" | custom-call | flops 400000000 | bytes 2000000 | tf_op jit(solution)/shard_map/solve/pallas_call | solution.py:359
  (11 shorter events, 0.1 us)
Async XLA Ops:
  0.6 8.6 %collective-permute-start = (bf16[512,128]{1,0:T(8,128)(2,1)}, bf16[512,128]{1,0:T(8,128)(2,1)S(1)}, u32[]{:S(2)}, u32[]{:S(2)}) collective-permute-start(bf16[512,128]{1,0:T(8,128)(2,1)} %param.4), channel_id=1, source_target_pairs={{1,0},{0,1},{3,2},{2,3},{5,4},{4,5},{7,6},{6,7},{9,8},{8,9},{11,10... | collective-permute-start | bytes 393224 | tf_op jit(solution)/shard_map/ppermute | solution.py:288
  0.8 3.6 %copy-start.2 = (bf16[1,32,512]{2,1,0:T(8,128)(2,1)S(1)}, bf16[1,32,512]{2,1,0:T(8,128)(2,1)}, u32[]{:S(2)}) copy-start(bf16[1,32,512]{2,1,0:T(8,128)(2,1)} %param.5) | copy-start | bytes 98308
  0.8 8.4 %copy-start.1 = (bf16[512,128]{1,0:T(8,128)(2,1)S(1)}, bf16[512,128]{1,0:T(8,128)(2,1)}, u32[]{:S(2)}) copy-start(bf16[512,128]{1,0:T(8,128)(2,1)} %param.4) | copy-start | bytes 393220
  1.7 7.5 %collective-permute-start.1 = (bf16[256,128]{1,0:T(8,128)(2,1)S(1)}, bf16[256,128]{1,0:T(8,128)(2,1)S(1)}, u32[]{:S(2)}, u32[]{:S(2)}) collective-permute-start(bf16[256,128]{1,0:T(8,128)(2,1)S(1)} %constant_dynamic-slice_fusion), channel_id=1, source_target_pairs={{2,0},{3,1},{0,2},{1,3},{6,4},{7,5},{4,6},{5,7},{10,8},{11,9},{8,1... | collective-permute-start | bytes 196616 | tf_op jit(solution)/shard_map/ppermute | solution.py:286
  4.3 4.9 %collective-permute-start.2 = (bf16[256,128]{1,0:T(8,128)(2,1)S(1)}, bf16[256,128]{1,0:T(8,128)(2,1)S(1)}, u32[]{:S(2)}, u32[]{:S(2)}) collective-permute-start(bf16[256,128]{1,0:T(8,128)(2,1)S(1)} %constant_dynamic-slice_fusion), channel_id=1, source_target_pairs={{3,0},{2,1},{1,2},{0,3},{7,4},{6,5},{5,6},{4,7},{11,8},{10,9},{9,1... | collective-permute-start | bytes 196616 | tf_op jit(solution)/shard_map/ppermute | solution.py:287
  4.3 3.3 %collective-permute-start.3 = (bf16[32,512]{1,0:T(8,128)(2,1)S(1)}, bf16[32,512]{1,0:T(8,128)(2,1)S(1)}, u32[]{:S(2)}, u32[]{:S(2)}) collective-permute-start(bf16[32,512]{1,0:T(8,128)(2,1)S(1)} %bitcast.2), channel_id=1, source_target_pairs={{4,0},{0,4},{12,8},{8,12},{20,16},{16,20},{28,24},{24,28},{5,1},{1... | collective-permute-start | bytes 98312 | tf_op jit(solution)/shard_map/ppermute | solution.py:327
  6.1 0.7 %copy-start.3 = (s32[1,2]{1,0:T(1,128)S(1)}, s32[1,2]{1,0:T(1,128)}, u32[]{:S(2)}) copy-start(s32[1,2]{1,0:T(1,128)} %param.6) | copy-start | bytes 28
  7.6 5.0 %collective-permute-start.4 = (bf16[64,512]{1,0:T(8,128)(2,1)S(1)}, bf16[64,512]{1,0:T(8,128)(2,1)S(1)}, u32[]{:S(2)}, u32[]{:S(2)}) collective-permute-start(bf16[64,512]{1,0:T(8,128)(2,1)S(1)} %constant_dynamic-update-slice_fusion), channel_id=1, source_target_pairs={{8,0},{12,4},{0,8},{4,12},{24,16},{28,20},{16,24},{20,28},{9,1},{1... | collective-permute-start | bytes 196616 | tf_op jit(solution)/shard_map/ppermute | solution.py:327
  12.7 18.2 %collective-permute-start.5 = (bf16[128,512]{1,0:T(8,128)(2,1)S(1)}, bf16[128,512]{1,0:T(8,128)(2,1)S(1)}, u32[]{:S(2)}, u32[]{:S(2)}) collective-permute-start(bf16[128,512]{1,0:T(8,128)(2,1)S(1)} %compare_select_fusion.refs_2_), channel_id=1, source_target_pairs={{16,0},{20,4},{24,8},{28,12},{0,16},{4,20},{8,24},{12,28},{17,1},{... | collective-permute-start | bytes 393224 | tf_op jit(solution)/shard_map/ppermute | solution.py:333
  15.1 15.8 %collective-permute-start.6 = (bf16[128,512]{1,0:T(8,128)(2,1)S(1)}, bf16[128,512]{1,0:T(8,128)(2,1)S(1)}, u32[]{:S(2)}, u32[]{:S(2)}) collective-permute-start(bf16[128,512]{1,0:T(8,128)(2,1)S(1)} %compare_select_fusion.refs_2_), channel_id=1, source_target_pairs={{0,0},{4,1},{8,2},{12,3},{16,4},{20,5},{24,6},{28,7},{1,8},{5,9},{... | collective-permute-start | bytes 393224 | tf_op jit(solution)/shard_map/ppermute | solution.py:321
  19.0 11.9 %copy-start = (bf16[256,128]{1,0:T(8,128)(2,1)S(1)}, bf16[256,128]{1,0:T(8,128)(2,1)}, u32[]{:S(2)}) copy-start(bf16[256,128]{1,0:T(8,128)(2,1)} %refs_5_.1) | copy-start | bytes 196612
where the time goes:
time: 32.6 us; the launch traced here: 32.4 us
  Pallas kernels  16.7 us (51%)
  starting transfers between devices  12.3 us (38%)
  local copies, waits for them, and re-layouts  1.59 us (5%)
  waiting for transfers between devices  0.76 us (2%)
  between operations  0.7 us (2%)
    pallas_call x1, Pallas kernels, body(): pl.pallas_call(functools.partial(rest_kernel, 'row'), out_shape=(jax.Shap...  11.9 us
    ppermute x1, starting transfers between devices, to_side(): return lax.ppermute(array, ('col', 'row'), pairs)  3.9 us
    pallas_call x1, Pallas kernels, body(): pl.pallas_call(functools.partial(first_kernel, 'row'), out_shape=(jax.Sha...  3.4 us
    ppermute x2, starting transfers between devices, body(): lax.ppermute(quad, 'col', [(d ^ step, d) for d in range(cols)])  3.22 us
    ppermute x1, starting transfers between devices, body(): far = lax.ppermute(diagonal_half, 'row', [(d ^ 2, d) for d in range(rows)])  2.66 us
    ppermute x1, starting transfers between devices, body(): lax.ppermute(quad, 'col', [(d ^ rows, d) for d in range(cols)])  2.37 us
    pallas_call x1, Pallas kernels, body(): pl.pallas_call(functools.partial(solve_kernel, 'row', 'col', True if pair...  1.45 us
    dynamic_slice x1, local copies, waits for them, and re-layouts, body(): lax.dynamic_slice_in_dim(pivot_block, row_index // 2 * half, half, 0)  0.92 us
  transfers between devices with their start and end apart: 7, of which 1 were waited for; matrix products, arithmetic and copies ran while one was open for 3% of the time, Pallas kernels for 47%

commit v1 on v0

--- a/solution.py
+++ b/solution.py
@@ -59,8 +59,9 @@
         guess, correction = reciprocal(det)
         n1 = [None if g < home else c * u[g] - b * v[g] for g in range(groups)]
         n2 = [None if g < home else a * v[g] - b * u[g] for g in range(groups)]
-        w1 = [None if g < home else (n1[g] * guess) * correction for g in range(groups)]
-        w2 = [None if g < home else (n2[g] * guess) * correction for g in range(groups)]
+        inverse = guess * correction
+        w1 = [None if g < home else n1[g] * inverse for g in range(groups)]
+        w2 = [None if g < home else n2[g] * inverse for g in range(groups)]
         for j in range(k + 2, last):
             at, row = j // GROUP, j % GROUP
             uj, vj = row_of(u[at], row), row_of(v[at], row)
@@ -75,12 +76,13 @@
         for g in range(home, groups):
             lower[g] = jnp.where(lane == first + k, u[g] * root_a, lower[g])
             lower[g] = jnp.where(lane == first + k + 1, n2[g] * root_d, lower[g])
-        below = sublane > sub + 1
-        w1[home] = jnp.where(below, w1[home], 0.0)
-        w2[home] = jnp.where(below, w2[home], 0.0)
         t0, t1 = row_of(block[home], sub), row_of(block[home], sub + 1)
         for g in range(home, groups):
-            block[g] = block[g] - (w1[g] * t0 + w2[g] * t1)
+            step = w1[g] * t0 + w2[g] * t1
+            if g > home:
+                block[g] = block[g] - step
+            elif sub + 2 < GROUP:
+                block[g] = block[g] - jnp.where(sublane > sub + 1, step, 0.0)
         block[home] = jnp.where(sublane == sub, t0 * root_a, block[home])
         block[home] = jnp.where(sublane == sub + 1, (a * t1 - b * t0) * root_d, block[home])
     for g in range(groups):
@@ -139,33 +141,37 @@
     return [jnp.concatenate(part, axis=0) for part in done]
 
 
-def assemble(me, own, mate, far, far_mate, work):
+def assemble(me, own, mate, far, far_mate, work, start, stop):
     size = own.shape[0]
     half = size // 2
     near = ((own, me), (mate, jnp.bitwise_xor(me, 1)))
     other = ((far, jnp.bitwise_xor(me, 2)), (far_mate, jnp.bitwise_xor(me, 3)))
 
+    def place(parts, low, high, offset):
+        low, high = max(low, start), min(high, stop)
+        for part, column in parts:
+            if low < high:
+                work[column, low:high, :] = part[low - offset : high - offset, :].astype(jnp.float32)
+
     @pl.when(me < 2)
     def _():
-        for part, column in near:
-            work[column, :half, :] = part[:half, :].astype(jnp.float32)
+        place(near, 0, half, 0)
+        place(other, half, size, half)
+        for row_block in range(start // LANES, min(half, stop) // LANES):
             for block in range(half // LANES, size // LANES):
-                flipped = part[block * LANES : (block + 1) * LANES, :].astype(jnp.float32).T
-                work[block, rows_at(column), :] = flipped
-        for part, column in other:
-            work[column, half:size, :] = part[...].astype(jnp.float32)
+                here = slice(block * LANES, (block + 1) * LANES)
+                flipped = jnp.where(me == row_block, own[here, :], mate[here, :].astype(jnp.float32)).T
+                work[block, row_block * LANES : (row_block + 1) * LANES, :] = flipped
 
     @pl.when(me >= 2)
     def _():
-        for part, column in near:
-            work[column, :size, :] = part[...].astype(jnp.float32)
-        for part, column in other:
-            work[column, :half, :] = part[...].astype(jnp.float32)
+        place(near, 0, size, 0)
+        place(other, 0, half, 0)
 
 
 def first_kernel(axis, own, mate, far, far_mate, done_ref, lower_ref, work):
     count = lax.axis_size(axis)
-    assemble(lax.axis_index(axis), own, mate, far, far_mate, work)
+    assemble(lax.axis_index(axis), own, mate, far, far_mate, work, 0, LANES)
     done = eliminate_block([work[d, :LANES, :] for d in range(count)], lower_ref)
     for d in range(count):
         done_ref[d] = done[d]
@@ -178,7 +184,7 @@
     me = lax.axis_index(axis)
     lane, row = square_iota(1), square_iota(0)
     beyond = beyond_strip()
-    assemble(me, own, mate, far, far_mate, work)
+    assemble(me, own, mate, far, far_mate, work, LANES, count * LANES)
     work[:count, :LANES, :] = done_ref[...]
     lower[0] = first_lower[...]
 
@@ -285,7 +291,8 @@
     diagonal_half = lax.dynamic_slice_in_dim(pivot_block, row_index // 2 * half, half, 0)
     far = lax.ppermute(diagonal_half, "row", [(d ^ 2, d) for d in range(rows)])
     far_mate = lax.ppermute(diagonal_half, "row", [(d ^ 3, d) for d in range(rows)])
-    mate = lax.ppermute(pivot_block, "row", [(d ^ 1, d) for d in range(rows)])
+    whole, _ = lax.optimization_barrier((pivot_block, diagonal_half))
+    mate = lax.ppermute(whole, "row", [(d ^ 1, d) for d in range(rows)])
     pivots = [wide, mate, far, far_mate]
 
     done, first_lower = pl.pallas_call(
@@ -296,7 +303,7 @@
         ),
         in_specs=[vmem] * len(pivots),
         out_specs=(vmem,) * 2,
-        scratch_shapes=[pltpu.VMEM((rows, pivot_size, LANES), jnp.float32)],
+        scratch_shapes=[pltpu.VMEM((rows, LANES, LANES), jnp.float32)],
         compiler_params=pltpu.CompilerParams(vmem_limit_bytes=32 * 1024 * 1024),
         cost_estimate=pl.CostEstimate(flops=3 * 10**8, bytes_accessed=10**6, transcendentals=10**5),
         name="first",

time: 32.6 us -> 32.6 us (level)
    ppermute x1, starting transfers between devices: 2.66 us -> 2.04 us  [body(): far = lax.ppermute(diagonal_half, 'row', [(d ^ 2, d) for d in range(rows)])]
    ppermute x1, starting transfers between devices: 0.01 us -> 0.59 us  [body(): lax.ppermute(diagonal_half, 'row', [(d ^ 3, d) for d in range(rows)])]
    ppermute x1, starting transfers between devices: 3.9 us -> 4.24 us  [to_side(): return lax.ppermute(array, ('col', 'row'), pairs)]
  transfers between devices with their start and end apart: 7 -> 7, of which waited for: 1 -> 1; matrix products, arithmetic and copies ran while one was open for 3% -> 1% of each run, Pallas kernels for 47% -> 46%
where the time goes in v1:
time: 32.6 us; the launch traced here: 32.4 us
  Pallas kernels  16.5 us (51%)
  starting transfers between devices  12.6 us (39%)
  local copies, waits for them, and re-layouts  1.56 us (5%)
  waiting for transfers between devices  0.77 us (2%)
  between operations  0.74 us (2%)
    pallas_call x1, Pallas kernels, body(): pl.pallas_call(functools.partial(rest_kernel, 'row'), out_shape=(jax.Shap...  11.7 us
    ppermute x1, starting transfers between devices, to_side(): return lax.ppermute(array, ('col', 'row'), pairs)  4.24 us
    pallas_call x1, Pallas kernels, body(): pl.pallas_call(functools.partial(first_kernel, 'row'), out_shape=(jax.Sha...  3.32 us
    ppermute x2, starting transfers between devices, body(): lax.ppermute(quad, 'col', [(d ^ step, d) for d in range(cols)])  2.95 us
    ppermute x1, starting transfers between devices, body(): lax.ppermute(quad, 'col', [(d ^ rows, d) for d in range(cols)])  2.37 us
    ppermute x1, starting transfers between devices, body(): far = lax.ppermute(diagonal_half, 'row', [(d ^ 2, d) for d in range(rows)])  2.04 us
    pallas_call x1, Pallas kernels, body(): pl.pallas_call(functools.partial(solve_kernel, 'row', 'col', True if pair...  1.45 us
    dynamic_slice x1, local copies, waits for them, and re-layouts, body(): lax.dynamic_slice_in_dim(pivot_block, row_index // 2 * half, half, 0)  0.88 us
  transfers between devices with their start and end apart: 7, of which 1 were waited for; matrix products, arithmetic and copies ran while one was open for 1% of the time, Pallas kernels for 46%

profile of v1, /device:TPU:1, one launch (start us, length us, event | category | flops | bytes accessed | tf_op | source)
XLA Modules:
  0.0 32.4 jit_solution(825115631689045308)
XLA Ops:
  0.6 0.0 copy-start.1
  0.7 0.9 %constant_dynamic-slice_fusion = bf16[256,128]{1,0:T(8,128)(2,1)S(1)} fusion(bf16[512,128]{1,0:T(8,128)(2,1)} %param.4, s32[]{:T(128)S(6)} %select_n.40), kind=kLoop, calls=%fused_computation.29 | loop fusion | bytes 131076 | tf_op jit(solution)/shard_map/dynamic_slice | solution.py:291
  1.6 2.0 %collective-permute-start.1 = (bf16[256,128]{1,0:T(8,128)(2,1)S(1)}, bf16[256,128]{1,0:T(8,128)(2,1)S(1)}, u32[]{:S(2)}, u32[]{:S(2)}) collective-permute-start(bf16[256,128]{1,0:T(8,128)(2,1)S(1)} %constant_dynamic-slice_fusion), channel_id=1, source_target_pairs={{2,0},{3,1},{0,2},{1,3},{6,4},{7,5},{4,6},{5,7},{10,8},{11,9},{8,1... | collective-permute-start | bytes 196616 | tf_op jit(solution)/shard_map/ppermute | solution.py:292
  3.6 0.6 %collective-permute-start.2 = (bf16[256,128]{1,0:T(8,128)(2,1)S(1)}, bf16[256,128]{1,0:T(8,128)(2,1)S(1)}, u32[]{:S(2)}, u32[]{:S(2)}) collective-permute-start(bf16[256,128]{1,0:T(8,128)(2,1)S(1)} %constant_dynamic-slice_fusion), channel_id=1, source_target_pairs={{3,0},{2,1},{1,2},{0,3},{7,4},{6,5},{5,6},{4,7},{11,8},{10,9},{9,1... | collective-permute-start | bytes 196616 | tf_op jit(solution)/shard_map/ppermute | solution.py:293
  4.2 0.4 %collective-permute-start = (bf16[512,128]{1,0:T(8,128)(2,1)S(1)}, bf16[512,128]{1,0:T(8,128)(2,1)S(1)}, u32[]{:S(2)}, u32[]{:S(2)}) collective-permute-start(bf16[512,128]{1,0:T(8,128)(2,1)S(1)} %copy-done.1), channel_id=1, source_target_pairs={{1,0},{0,1},{3,2},{2,3},{5,4},{4,5},{7,6},{6,7},{9,8},{8,9},{11,10... | collective-permute-start | bytes 393224 | tf_op jit(solution)/shard_map/ppermute | solution.py:295
  4.6 1.4 %collective-permute-start.3 = (bf16[32,512]{1,0:T(8,128)(2,1)S(1)}, bf16[32,512]{1,0:T(8,128)(2,1)S(1)}, u32[]{:S(2)}, u32[]{:S(2)}) collective-permute-start(bf16[32,512]{1,0:T(8,128)(2,1)S(1)} %bitcast.2), channel_id=1, source_target_pairs={{4,0},{0,4},{12,8},{8,12},{20,16},{16,20},{28,24},{24,28},{5,1},{1... | collective-permute-start | bytes 98312 | tf_op jit(solution)/shard_map/ppermute | solution.py:334
  6.0 0.1 pad_add_fusion
  6.1 0.7 %copy-done.3 = s32[1,2]{1,0:T(1,128)S(1)} copy-done((s32[1,2]{1,0:T(1,128)S(1)}, s32[1,2]{1,0:T(1,128)}, u32[]{:S(2)}) %copy-start.3) | copy-done | bytes 32
  6.8 0.1 fusion.3
  6.9 0.8 %collective-permute-done.3 = bf16[32,512]{1,0:T(8,128)(2,1)S(1)} collective-permute-done((bf16[32,512]{1,0:T(8,128)(2,1)S(1)}, bf16[32,512]{1,0:T(8,128)(2,1)S(1)}, u32[]{:S(2)}, u32[]{:S(2)}) %collective-permute-start.3) | collective-permute-done | bytes 32800 | tf_op jit(solution)/shard_map/ppermute | solution.py:334
  7.6 1.5 %collective-permute-start.4 = (bf16[64,512]{1,0:T(8,128)(2,1)S(1)}, bf16[64,512]{1,0:T(8,128)(2,1)S(1)}, u32[]{:S(2)}, u32[]{:S(2)}) collective-permute-start(bf16[64,512]{1,0:T(8,128)(2,1)S(1)} %constant_dynamic-update-slice_fusion), channel_id=1, source_target_pairs={{8,0},{12,4},{0,8},{4,12},{24,16},{28,20},{16,24},{20,28},{9,1},{1... | collective-permute-start | bytes 196616 | tf_op jit(solution)/shard_map/ppermute | solution.py:334
  9.2 0.0 collective-permute-done.1.far
  9.2 0.0 collective-permute-done.2.far_mate
  9.2 0.0 collective-permute-done.mate
  9.2 3.3 %first.1 = (f32[4,128,128]{2,1,0:T(8,128)S(1)}, f32[128,128]{1,0:T(8,128)S(1)}) custom-call(f32[512,128]{1,0:T(8,128)S(1)} %convert_element_type.3.own, bf16[512,128]{1,0:T(8,128)(2,1)S(1)} %collective-permute-done.mate, bf16[256,128]{1,0:T(8,128)(2,1)S(1)} %collective-permute-done.1.far, bf16[256,128]{1,0:T(8,128)(2,1)S(1)} %collective-permute-done.2.far_mate), custom_call_target="tpu_custom_call" | custom-call | flops 300000000 | bytes 1000000 | tf_op jit(solution)/shard_map/first/pallas_call | solution.py:298
  12.5 0.0 collective-permute-done.4
  12.5 0.1 compare_select_fusion.refs_2_
  12.6 2.4 %collective-permute-start.5 = (bf16[128,512]{1,0:T(8,128)(2,1)S(1)}, bf16[128,512]{1,0:T(8,128)(2,1)S(1)}, u32[]{:S(2)}, u32[]{:S(2)}) collective-permute-start(bf16[128,512]{1,0:T(8,128)(2,1)S(1)} %compare_select_fusion.refs_2_), channel_id=1, source_target_pairs={{16,0},{20,4},{24,8},{28,12},{0,16},{4,20},{8,24},{12,28},{17,1},{... | collective-permute-start | bytes 393224 | tf_op jit(solution)/shard_map/ppermute | solution.py:340
  15.0 4.2 %collective-permute-start.6 = (bf16[128,512]{1,0:T(8,128)(2,1)S(1)}, bf16[128,512]{1,0:T(8,128)(2,1)S(1)}, u32[]{:S(2)}, u32[]{:S(2)}) collective-permute-start(bf16[128,512]{1,0:T(8,128)(2,1)S(1)} %compare_select_fusion.refs_2_), channel_id=1, source_target_pairs={{0,0},{4,1},{8,2},{12,3},{16,4},{20,5},{24,6},{28,7},{1,8},{5,9},{... | collective-permute-start | bytes 393224 | tf_op jit(solution)/shard_map/ppermute | solution.py:328
  19.2 0.0 copy-start
  19.2 11.7 %rest.1 = (f32[512,128]{1,0:T(8,128)}, bf16[512,512]{1,0:T(8,128)(2,1)S(1)}, bf16[512,512]{1,0:T(8,128)(2,1)S(1)}) custom-call(f32[512,128]{1,0:T(8,128)S(1)} %convert_element_type.3.own, bf16[512,128]{1,0:T(8,128)(2,1)S(1)} %collective-permute-done.mate, bf16[256,128]{1,0:T(8,128)(2,1)S(1)} %collective-permute-done.1.far, ...), custom_call_target="tpu_custom_call" | custom-call | flops 1000000000 | bytes 2000000 | tf_op jit(solution)/shard_map/rest/pallas_call | solution.py:347
  31.0 0.0 collective-permute-done.5.refs_3_
  31.0 0.0 collective-permute-done.6.refs_4_
  31.0 1.4 %solve.1 = (bf16[1,32,512]{2,1,0:T(8,128)(2,1)}, bf16[256,128]{1,0:T(8,128)(2,1)}) custom-call(bf16[512,512]{1,0:T(8,128)(2,1)S(1)} %get-tuple-element.18.refs_0_, bf16[512,512]{1,0:T(8,128)(2,1)S(1)} %get-tuple-element.19.refs_1_, bf16[128,512]{1,0:T(8,128)(2,1)S(1)} %compare_select_fusion.refs_2_, bf16[128,512]{1,0:T(8,128)(2,1)S(1)} %collective-permute-done.5.refs_3_, ...), custom_call_target="tpu_custom_call" | custom-call | flops 400000000 | bytes 2000000 | tf_op jit(solution)/shard_map/solve/pallas_call | solution.py:366
  (11 shorter events, 0.1 us)
Async XLA Ops:
  0.6 3.6 %copy-start.1 = (bf16[512,128]{1,0:T(8,128)(2,1)S(1)}, bf16[512,128]{1,0:T(8,128)(2,1)}, u32[]{:S(2)}) copy-start(bf16[512,128]{1,0:T(8,128)(2,1)} %param.4) | copy-start | bytes 393220
  0.7 3.9 %copy-start.2 = (bf16[1,32,512]{2,1,0:T(8,128)(2,1)S(1)}, bf16[1,32,512]{2,1,0:T(8,128)(2,1)}, u32[]{:S(2)}) copy-start(bf16[1,32,512]{2,1,0:T(8,128)(2,1)} %param.5) | copy-start | bytes 98308
  1.6 7.6 %collective-permute-start.1 = (bf16[256,128]{1,0:T(8,128)(2,1)S(1)}, bf16[256,128]{1,0:T(8,128)(2,1)S(1)}, u32[]{:S(2)}, u32[]{:S(2)}) collective-permute-start(bf16[256,128]{1,0:T(8,128)(2,1)S(1)} %constant_dynamic-slice_fusion), channel_id=1, source_target_pairs={{2,0},{3,1},{0,2},{1,3},{6,4},{7,5},{4,6},{5,7},{10,8},{11,9},{8,1... | collective-permute-start | bytes 196616 | tf_op jit(solution)/shard_map/ppermute | solution.py:292
  3.6 5.6 %collective-permute-start.2 = (bf16[256,128]{1,0:T(8,128)(2,1)S(1)}, bf16[256,128]{1,0:T(8,128)(2,1)S(1)}, u32[]{:S(2)}, u32[]{:S(2)}) collective-permute-start(bf16[256,128]{1,0:T(8,128)(2,1)S(1)} %constant_dynamic-slice_fusion), channel_id=1, source_target_pairs={{3,0},{2,1},{1,2},{0,3},{7,4},{6,5},{5,6},{4,7},{11,8},{10,9},{9,1... | collective-permute-start | bytes 196616 | tf_op jit(solution)/shard_map/ppermute | solution.py:293
  4.2 5.0 %collective-permute-start = (bf16[512,128]{1,0:T(8,128)(2,1)S(1)}, bf16[512,128]{1,0:T(8,128)(2,1)S(1)}, u32[]{:S(2)}, u32[]{:S(2)}) collective-permute-start(bf16[512,128]{1,0:T(8,128)(2,1)S(1)} %copy-done.1), channel_id=1, source_target_pairs={{1,0},{0,1},{3,2},{2,3},{5,4},{4,5},{7,6},{6,7},{9,8},{8,9},{11,10... | collective-permute-start | bytes 393224 | tf_op jit(solution)/shard_map/ppermute | solution.py:295
  4.6 3.1 %collective-permute-start.3 = (bf16[32,512]{1,0:T(8,128)(2,1)S(1)}, bf16[32,512]{1,0:T(8,128)(2,1)S(1)}, u32[]{:S(2)}, u32[]{:S(2)}) collective-permute-start(bf16[32,512]{1,0:T(8,128)(2,1)S(1)} %bitcast.2), channel_id=1, source_target_pairs={{4,0},{0,4},{12,8},{8,12},{20,16},{16,20},{28,24},{24,28},{5,1},{1... | collective-permute-start | bytes 98312 | tf_op jit(solution)/shard_map/ppermute | solution.py:334
  6.1 0.7 %copy-start.3 = (s32[1,2]{1,0:T(1,128)S(1)}, s32[1,2]{1,0:T(1,128)}, u32[]{:S(2)}) copy-start(s32[1,2]{1,0:T(1,128)} %param.6) | copy-start | bytes 28
  7.6 4.9 %collective-permute-start.4 = (bf16[64,512]{1,0:T(8,128)(2,1)S(1)}, bf16[64,512]{1,0:T(8,128)(2,1)S(1)}, u32[]{:S(2)}, u32[]{:S(2)}) collective-permute-start(bf16[64,512]{1,0:T(8,128)(2,1)S(1)} %constant_dynamic-update-slice_fusion), channel_id=1, source_target_pairs={{8,0},{12,4},{0,8},{4,12},{24,16},{28,20},{16,24},{20,28},{9,1},{1... | collective-permute-start | bytes 196616 | tf_op jit(solution)/shard_map/ppermute | solution.py:334
  12.6 18.4 %collective-permute-start.5 = (bf16[128,512]{1,0:T(8,128)(2,1)S(1)}, bf16[128,512]{1,0:T(8,128)(2,1)S(1)}, u32[]{:S(2)}, u32[]{:S(2)}) collective-permute-start(bf16[128,512]{1,0:T(8,128)(2,1)S(1)} %compare_select_fusion.refs_2_), channel_id=1, source_target_pairs={{16,0},{20,4},{24,8},{28,12},{0,16},{4,20},{8,24},{12,28},{17,1},{... | collective-permute-start | bytes 393224 | tf_op jit(solution)/shard_map/ppermute | solution.py:340
  15.0 16.0 %collective-permute-start.6 = (bf16[128,512]{1,0:T(8,128)(2,1)S(1)}, bf16[128,512]{1,0:T(8,128)(2,1)S(1)}, u32[]{:S(2)}, u32[]{:S(2)}) collective-permute-start(bf16[128,512]{1,0:T(8,128)(2,1)S(1)} %compare_select_fusion.refs_2_), channel_id=1, source_target_pairs={{0,0},{4,1},{8,2},{12,3},{16,4},{20,5},{24,6},{28,7},{1,8},{5,9},{... | collective-permute-start | bytes 393224 | tf_op jit(solution)/shard_map/ppermute | solution.py:328
  19.2 11.8 %copy-start = (bf16[256,128]{1,0:T(8,128)(2,1)S(1)}, bf16[256,128]{1,0:T(8,128)(2,1)}, u32[]{:S(2)}) copy-start(bf16[256,128]{1,0:T(8,128)(2,1)} %refs_5_.1) | copy-start | bytes 196612

commit v2 on v1

--- a/solution.py
+++ b/solution.py
@@ -291,8 +291,7 @@
     diagonal_half = lax.dynamic_slice_in_dim(pivot_block, row_index // 2 * half, half, 0)
     far = lax.ppermute(diagonal_half, "row", [(d ^ 2, d) for d in range(rows)])
     far_mate = lax.ppermute(diagonal_half, "row", [(d ^ 3, d) for d in range(rows)])
-    whole, _ = lax.optimization_barrier((pivot_block, diagonal_half))
-    mate = lax.ppermute(whole, "row", [(d ^ 1, d) for d in range(rows)])
+    mate = lax.ppermute(pivot_block, "row", [(d ^ 1, d) for d in range(rows)])
     pivots = [wide, mate, far, far_mate]
 
     done, first_lower = pl.pallas_call(

time: 32.6 us -> 32.4 us (level)
    ppermute x1, starting transfers between devices: 2.04 us -> 2.66 us  [body(): far = lax.ppermute(diagonal_half, 'row', [(d ^ 2, d) for d in range(rows)])]
    ppermute x1, starting transfers between devices: 0.59 us -> 0.01 us  [body(): lax.ppermute(diagonal_half, 'row', [(d ^ 3, d) for d in range(rows)])]
  transfers between devices with their start and end apart: 7 -> 7, of which waited for: 1 -> 1; matrix products, arithmetic and copies ran while one was open for 1% -> 4% of each run, Pallas kernels for 46% -> 47%
where the time goes in v2:
time: 32.4 us; the launch traced here: 32.2 us
  Pallas kernels  16.5 us (51%)
  starting transfers between devices  12.4 us (38%)
  local copies, waits for them, and re-layouts  1.59 us (5%)
  waiting for transfers between devices  0.76 us (2%)
  between operations  0.7 us (2%)
    pallas_call x1, Pallas kernels, body(): pl.pallas_call(functools.partial(rest_kernel, 'row'), out_shape=(jax.Shap...  11.7 us
    ppermute x1, starting transfers between devices, to_side(): return lax.ppermute(array, ('col', 'row'), pairs)  3.98 us
    pallas_call x1, Pallas kernels, body(): pl.pallas_call(functools.partial(first_kernel, 'row'), out_shape=(jax.Sha...  3.32 us
    ppermute x2, starting transfers between devices, body(): lax.ppermute(quad, 'col', [(d ^ step, d) for d in range(cols)])  3.22 us
    ppermute x1, starting transfers between devices, body(): far = lax.ppermute(diagonal_half, 'row', [(d ^ 2, d) for d in range(rows)])  2.66 us
    ppermute x1, starting transfers between devices, body(): lax.ppermute(quad, 'col', [(d ^ rows, d) for d in range(cols)])  2.37 us
    pallas_call x1, Pallas kernels, body(): pl.pallas_call(functools.partial(solve_kernel, 'row', 'col', True if pair...  1.45 us
    dynamic_slice x1, local copies, waits for them, and re-layouts, body(): lax.dynamic_slice_in_dim(pivot_block, row_index // 2 * half, half, 0)  0.92 us
  transfers between devices with their start and end apart: 7, of which 1 were waited for; matrix products, arithmetic and copies ran while one was open for 4% of the time, Pallas kernels for 47%

profile of v2, /device:TPU:1, one launch (start us, length us, event | category | flops | bytes accessed | tf_op | source)
XLA Modules:
  0.0 32.2 jit_solution(10893555057797219155)
XLA Ops:
  0.6 0.1 collective-permute-start
  0.8 0.9 %constant_dynamic-slice_fusion = bf16[256,128]{1,0:T(8,128)(2,1)S(1)} fusion(bf16[512,128]{1,0:T(8,128)(2,1)} %param.4, s32[]{:T(128)S(6)} %select_n.40), kind=kLoop, calls=%fused_computation.29 | loop fusion | bytes 131076 | tf_op jit(solution)/shard_map/dynamic_slice | solution.py:291
  1.7 2.7 %collective-permute-start.1 = (bf16[256,128]{1,0:T(8,128)(2,1)S(1)}, bf16[256,128]{1,0:T(8,128)(2,1)S(1)}, u32[]{:S(2)}, u32[]{:S(2)}) collective-permute-start(bf16[256,128]{1,0:T(8,128)(2,1)S(1)} %constant_dynamic-slice_fusion), channel_id=1, source_target_pairs={{2,0},{3,1},{0,2},{1,3},{6,4},{7,5},{4,6},{5,7},{10,8},{11,9},{8,1... | collective-permute-start | bytes 196616 | tf_op jit(solution)/shard_map/ppermute | solution.py:292
  4.3 0.0 collective-permute-start.2
  4.3 0.0 copy-done.2
  4.3 1.7 %collective-permute-start.3 = (bf16[32,512]{1,0:T(8,128)(2,1)S(1)}, bf16[32,512]{1,0:T(8,128)(2,1)S(1)}, u32[]{:S(2)}, u32[]{:S(2)}) collective-permute-start(bf16[32,512]{1,0:T(8,128)(2,1)S(1)} %bitcast.2), channel_id=1, source_target_pairs={{4,0},{0,4},{12,8},{8,12},{20,16},{16,20},{28,24},{24,28},{5,1},{1... | collective-permute-start | bytes 98312 | tf_op jit(solution)/shard_map/ppermute | solution.py:333
  6.1 0.1 pad_add_fusion
  6.1 0.7 %copy-done.3 = s32[1,2]{1,0:T(1,128)S(1)} copy-done((s32[1,2]{1,0:T(1,128)S(1)}, s32[1,2]{1,0:T(1,128)}, u32[]{:S(2)}) %copy-start.3) | copy-done | bytes 32
  6.8 0.1 fusion.3
  6.9 0.7 %collective-permute-done.3 = bf16[32,512]{1,0:T(8,128)(2,1)S(1)} collective-permute-done((bf16[32,512]{1,0:T(8,128)(2,1)S(1)}, bf16[32,512]{1,0:T(8,128)(2,1)S(1)}, u32[]{:S(2)}, u32[]{:S(2)}) %collective-permute-start.3) | collective-permute-done | bytes 32800 | tf_op jit(solution)/shard_map/ppermute | solution.py:333
  7.6 1.5 %collective-permute-start.4 = (bf16[64,512]{1,0:T(8,128)(2,1)S(1)}, bf16[64,512]{1,0:T(8,128)(2,1)S(1)}, u32[]{:S(2)}, u32[]{:S(2)}) collective-permute-start(bf16[64,512]{1,0:T(8,128)(2,1)S(1)} %constant_dynamic-update-slice_fusion), channel_id=1, source_target_pairs={{8,0},{12,4},{0,8},{4,12},{24,16},{28,20},{16,24},{20,28},{9,1},{1... | collective-permute-start | bytes 196616 | tf_op jit(solution)/shard_map/ppermute | solution.py:333
  9.2 0.0 collective-permute-done.1.far
  9.2 0.0 collective-permute-done.2.far_mate
  9.2 0.0 collective-permute-done.mate
  9.2 3.3 %first.1 = (f32[4,128,128]{2,1,0:T(8,128)S(1)}, f32[128,128]{1,0:T(8,128)S(1)}) custom-call(f32[512,128]{1,0:T(8,128)S(1)} %convert_element_type.3.own, bf16[512,128]{1,0:T(8,128)(2,1)S(1)} %collective-permute-done.mate, bf16[256,128]{1,0:T(8,128)(2,1)S(1)} %collective-permute-done.1.far, bf16[256,128]{1,0:T(8,128)(2,1)S(1)} %collective-permute-done.2.far_mate), custom_call_target="tpu_custom_call" | custom-call | flops 300000000 | bytes 1000000 | tf_op jit(solution)/shard_map/first/pallas_call | solution.py:297
  12.5 0.0 collective-permute-done.4
  12.5 0.1 compare_select_fusion.refs_2_
  12.6 2.4 %collective-permute-start.5 = (bf16[128,512]{1,0:T(8,128)(2,1)S(1)}, bf16[128,512]{1,0:T(8,128)(2,1)S(1)}, u32[]{:S(2)}, u32[]{:S(2)}) collective-permute-start(bf16[128,512]{1,0:T(8,128)(2,1)S(1)} %compare_select_fusion.refs_2_), channel_id=1, source_target_pairs={{16,0},{20,4},{24,8},{28,12},{0,16},{4,20},{8,24},{12,28},{17,1},{... | collective-permute-start | bytes 393224 | tf_op jit(solution)/shard_map/ppermute | solution.py:339
  15.0 4.0 %collective-permute-start.6 = (bf16[128,512]{1,0:T(8,128)(2,1)S(1)}, bf16[128,512]{1,0:T(8,128)(2,1)S(1)}, u32[]{:S(2)}, u32[]{:S(2)}) collective-permute-start(bf16[128,512]{1,0:T(8,128)(2,1)S(1)} %compare_select_fusion.refs_2_), channel_id=1, source_target_pairs={{0,0},{4,1},{8,2},{12,3},{16,4},{20,5},{24,6},{28,7},{1,8},{5,9},{... | collective-permute-start | bytes 393224 | tf_op jit(solution)/shard_map/ppermute | solution.py:327
  19.0 0.0 copy-start
  19.0 11.7 %rest.1 = (f32[512,128]{1,0:T(8,128)}, bf16[512,512]{1,0:T(8,128)(2,1)S(1)}, bf16[512,512]{1,0:T(8,128)(2,1)S(1)}) custom-call(f32[512,128]{1,0:T(8,128)S(1)} %convert_element_type.3.own, bf16[512,128]{1,0:T(8,128)(2,1)S(1)} %collective-permute-done.mate, bf16[256,128]{1,0:T(8,128)(2,1)S(1)} %collective-permute-done.1.far, ...), custom_call_target="tpu_custom_call" | custom-call | flops 1000000000 | bytes 2000000 | tf_op jit(solution)/shard_map/rest/pallas_call | solution.py:346
  30.8 0.0 collective-permute-done.5.refs_3_
  30.8 0.0 collective-permute-done.6.refs_4_
  30.8 1.4 %solve.1 = (bf16[1,32,512]{2,1,0:T(8,128)(2,1)}, bf16[256,128]{1,0:T(8,128)(2,1)}) custom-call(bf16[512,512]{1,0:T(8,128)(2,1)S(1)} %get-tuple-element.16.refs_0_, bf16[512,512]{1,0:T(8,128)(2,1)S(1)} %get-tuple-element.17.refs_1_, bf16[128,512]{1,0:T(8,128)(2,1)S(1)} %compare_select_fusion.refs_2_, bf16[128,512]{1,0:T(8,128)(2,1)S(1)} %collective-permute-done.5.refs_3_, ...), custom_call_target="tpu_custom_call" | custom-call | flops 400000000 | bytes 2000000 | tf_op jit(solution)/shard_map/solve/pallas_call | solution.py:365
  (11 shorter events, 0.1 us)
Async XLA Ops:
  0.6 8.6 %collective-permute-start = (bf16[512,128]{1,0:T(8,128)(2,1)}, bf16[512,128]{1,0:T(8,128)(2,1)S(1)}, u32[]{:S(2)}, u32[]{:S(2)}) collective-permute-start(bf16[512,128]{1,0:T(8,128)(2,1)} %param.4), channel_id=1, source_target_pairs={{1,0},{0,1},{3,2},{2,3},{5,4},{4,5},{7,6},{6,7},{9,8},{8,9},{11,10... | collective-permute-start | bytes 393224 | tf_op jit(solution)/shard_map/ppermute | solution.py:294
  0.8 3.6 %copy-start.2 = (bf16[1,32,512]{2,1,0:T(8,128)(2,1)S(1)}, bf16[1,32,512]{2,1,0:T(8,128)(2,1)}, u32[]{:S(2)}) copy-start(bf16[1,32,512]{2,1,0:T(8,128)(2,1)} %param.5) | copy-start | bytes 98308
  0.8 8.4 %copy-start.1 = (bf16[512,128]{1,0:T(8,128)(2,1)S(1)}, bf16[512,128]{1,0:T(8,128)(2,1)}, u32[]{:S(2)}) copy-start(bf16[512,128]{1,0:T(8,128)(2,1)} %param.4) | copy-start | bytes 393220
  1.7 7.5 %collective-permute-start.1 = (bf16[256,128]{1,0:T(8,128)(2,1)S(1)}, bf16[256,128]{1,0:T(8,128)(2,1)S(1)}, u32[]{:S(2)}, u32[]{:S(2)}) collective-permute-start(bf16[256,128]{1,0:T(8,128)(2,1)S(1)} %constant_dynamic-slice_fusion), channel_id=1, source_target_pairs={{2,0},{3,1},{0,2},{1,3},{6,4},{7,5},{4,6},{5,7},{10,8},{11,9},{8,1... | collective-permute-start | bytes 196616 | tf_op jit(solution)/shard_map/ppermute | solution.py:292
  4.3 4.9 %collective-permute-start.2 = (bf16[256,128]{1,0:T(8,128)(2,1)S(1)}, bf16[256,128]{1,0:T(8,128)(2,1)S(1)}, u32[]{:S(2)}, u32[]{:S(2)}) collective-permute-start(bf16[256,128]{1,0:T(8,128)(2,1)S(1)} %constant_dynamic-slice_fusion), channel_id=1, source_target_pairs={{3,0},{2,1},{1,2},{0,3},{7,4},{6,5},{5,6},{4,7},{11,8},{10,9},{9,1... | collective-permute-start | bytes 196616 | tf_op jit(solution)/shard_map/ppermute | solution.py:293
  4.3 3.3 %collective-permute-start.3 = (bf16[32,512]{1,0:T(8,128)(2,1)S(1)}, bf16[32,512]{1,0:T(8,128)(2,1)S(1)}, u32[]{:S(2)}, u32[]{:S(2)}) collective-permute-start(bf16[32,512]{1,0:T(8,128)(2,1)S(1)} %bitcast.2), channel_id=1, source_target_pairs={{4,0},{0,4},{12,8},{8,12},{20,16},{16,20},{28,24},{24,28},{5,1},{1... | collective-permute-start | bytes 98312 | tf_op jit(solution)/shard_map/ppermute | solution.py:333
  6.1 0.7 %copy-start.3 = (s32[1,2]{1,0:T(1,128)S(1)}, s32[1,2]{1,0:T(1,128)}, u32[]{:S(2)}) copy-start(s32[1,2]{1,0:T(1,128)} %param.6) | copy-start | bytes 28
  7.6 4.9 %collective-permute-start.4 = (bf16[64,512]{1,0:T(8,128)(2,1)S(1)}, bf16[64,512]{1,0:T(8,128)(2,1)S(1)}, u32[]{:S(2)}, u32[]{:S(2)}) collective-permute-start(bf16[64,512]{1,0:T(8,128)(2,1)S(1)} %constant_dynamic-update-slice_fusion), channel_id=1, source_target_pairs={{8,0},{12,4},{0,8},{4,12},{24,16},{28,20},{16,24},{20,28},{9,1},{1... | collective-permute-start | bytes 196616 | tf_op jit(solution)/shard_map/ppermute | solution.py:333
  12.6 18.1 %collective-permute-start.5 = (bf16[128,512]{1,0:T(8,128)(2,1)S(1)}, bf16[128,512]{1,0:T(8,128)(2,1)S(1)}, u32[]{:S(2)}, u32[]{:S(2)}) collective-permute-start(bf16[128,512]{1,0:T(8,128)(2,1)S(1)} %compare_select_fusion.refs_2_), channel_id=1, source_target_pairs={{16,0},{20,4},{24,8},{28,12},{0,16},{4,20},{8,24},{12,28},{17,1},{... | collective-permute-start | bytes 393224 | tf_op jit(solution)/shard_map/ppermute | solution.py:339
  15.0 15.8 %collective-permute-start.6 = (bf16[128,512]{1,0:T(8,128)(2,1)S(1)}, bf16[128,512]{1,0:T(8,128)(2,1)S(1)}, u32[]{:S(2)}, u32[]{:S(2)}) collective-permute-start(bf16[128,512]{1,0:T(8,128)(2,1)S(1)} %compare_select_fusion.refs_2_), channel_id=1, source_target_pairs={{0,0},{4,1},{8,2},{12,3},{16,4},{20,5},{24,6},{28,7},{1,8},{5,9},{... | collective-permute-start | bytes 393224 | tf_op jit(solution)/shard_map/ppermute | solution.py:327
  19.0 11.8 %copy-start = (bf16[256,128]{1,0:T(8,128)(2,1)S(1)}, bf16[256,128]{1,0:T(8,128)(2,1)}, u32[]{:S(2)}) copy-start(bf16[256,128]{1,0:T(8,128)(2,1)} %refs_5_.1) | copy-start | bytes 196612

commit v3 on v2

--- a/solution.py
+++ b/solution.py
@@ -67,7 +67,7 @@
             uj, vj = row_of(u[at], row), row_of(v[at], row)
             for g in range(at, groups):
                 if j < k + 4:
-                    step = ((n1[g] * uj + n2[g] * vj) * guess) * correction
+                    step = (n1[g] * uj + n2[g] * vj) * inverse
                 else:
                     step = w1[g] * uj + w2[g] * vj
                 column[j][g] = column[j][g] - step

time: 32.4 us -> 32.8 us (1.012)
  Pallas kernels: 16.5 us -> 16.9 us
  transfers between devices with their start and end apart: 7 -> 7, of which waited for: 1 -> 1; matrix products, arithmetic and copies ran while one was open for 4% -> 3% of each run, Pallas kernels for 47% -> 48%
where the time goes in v3:
time: 32.8 us; the launch traced here: 32.5 us
  Pallas kernels  16.9 us (52%)
  starting transfers between devices  12.2 us (37%)
  local copies, waits for them, and re-layouts  1.59 us (5%)
  waiting for transfers between devices  0.76 us (2%)
  between operations  0.7 us (2%)
    pallas_call x1, Pallas kernels, body(): pl.pallas_call(functools.partial(rest_kernel, 'row'), out_shape=(jax.Shap...  12.1 us
    ppermute x1, starting transfers between devices, to_side(): return lax.ppermute(array, ('col', 'row'), pairs)  3.87 us
    pallas_call x1, Pallas kernels, body(): pl.pallas_call(functools.partial(first_kernel, 'row'), out_shape=(jax.Sha...  3.42 us
    ppermute x2, starting transfers between devices, body(): lax.ppermute(quad, 'col', [(d ^ step, d) for d in range(cols)])  3.22 us
    ppermute x1, starting transfers between devices, body(): far = lax.ppermute(diagonal_half, 'row', [(d ^ 2, d) for d in range(rows)])  2.66 us
    ppermute x1, starting transfers between devices, body(): lax.ppermute(quad, 'col', [(d ^ rows, d) for d in range(cols)])  2.37 us
    pallas_call x1, Pallas kernels, body(): pl.pallas_call(functools.partial(solve_kernel, 'row', 'col', True if pair...  1.45 us
    dynamic_slice x1, local copies, waits for them, and re-layouts, body(): lax.dynamic_slice_in_dim(pivot_block, row_index // 2 * half, half, 0)  0.92 us
  transfers between devices with their start and end apart: 7, of which 1 were waited for; matrix products, arithmetic and copies ran while one was open for 3% of the time, Pallas kernels for 48%

profile of v3, /device:TPU:1, one launch (start us, length us, event | category | flops | bytes accessed | tf_op | source)
XLA Modules:
  0.0 32.5 jit_solution(15284866049583999604)
XLA Ops:
  0.6 0.1 collective-permute-start
  0.8 0.9 %constant_dynamic-slice_fusion = bf16[256,128]{1,0:T(8,128)(2,1)S(1)} fusion(bf16[512,128]{1,0:T(8,128)(2,1)} %param.4, s32[]{:T(128)S(6)} %select_n.40), kind=kLoop, calls=%fused_computation.29 | loop fusion | bytes 131076 | tf_op jit(solution)/shard_map/dynamic_slice | solution.py:291
  1.7 2.7 %collective-permute-start.1 = (bf16[256,128]{1,0:T(8,128)(2,1)S(1)}, bf16[256,128]{1,0:T(8,128)(2,1)S(1)}, u32[]{:S(2)}, u32[]{:S(2)}) collective-permute-start(bf16[256,128]{1,0:T(8,128)(2,1)S(1)} %constant_dynamic-slice_fusion), channel_id=1, source_target_pairs={{2,0},{3,1},{0,2},{1,3},{6,4},{7,5},{4,6},{5,7},{10,8},{11,9},{8,1... | collective-permute-start | bytes 196616 | tf_op jit(solution)/shard_map/ppermute | solution.py:292
  4.3 0.0 collective-permute-start.2
  4.3 0.0 copy-done.2
  4.3 1.7 %collective-permute-start.3 = (bf16[32,512]{1,0:T(8,128)(2,1)S(1)}, bf16[32,512]{1,0:T(8,128)(2,1)S(1)}, u32[]{:S(2)}, u32[]{:S(2)}) collective-permute-start(bf16[32,512]{1,0:T(8,128)(2,1)S(1)} %bitcast.2), channel_id=1, source_target_pairs={{4,0},{0,4},{12,8},{8,12},{20,16},{16,20},{28,24},{24,28},{5,1},{1... | collective-permute-start | bytes 98312 | tf_op jit(solution)/shard_map/ppermute | solution.py:333
  6.1 0.1 pad_add_fusion
  6.1 0.7 %copy-done.3 = s32[1,2]{1,0:T(1,128)S(1)} copy-done((s32[1,2]{1,0:T(1,128)S(1)}, s32[1,2]{1,0:T(1,128)}, u32[]{:S(2)}) %copy-start.3) | copy-done | bytes 32
  6.8 0.1 fusion.3
  6.9 0.7 %collective-permute-done.3 = bf16[32,512]{1,0:T(8,128)(2,1)S(1)} collective-permute-done((bf16[32,512]{1,0:T(8,128)(2,1)S(1)}, bf16[32,512]{1,0:T(8,128)(2,1)S(1)}, u32[]{:S(2)}, u32[]{:S(2)}) %collective-permute-start.3) | collective-permute-done | bytes 32800 | tf_op jit(solution)/shard_map/ppermute | solution.py:333
  7.6 1.5 %collective-permute-start.4 = (bf16[64,512]{1,0:T(8,128)(2,1)S(1)}, bf16[64,512]{1,0:T(8,128)(2,1)S(1)}, u32[]{:S(2)}, u32[]{:S(2)}) collective-permute-start(bf16[64,512]{1,0:T(8,128)(2,1)S(1)} %constant_dynamic-update-slice_fusion), channel_id=1, source_target_pairs={{8,0},{12,4},{0,8},{4,12},{24,16},{28,20},{16,24},{20,28},{9,1},{1... | collective-permute-start | bytes 196616 | tf_op jit(solution)/shard_map/ppermute | solution.py:333
  9.2 0.0 collective-permute-done.1.far
  9.2 0.0 collective-permute-done.2.far_mate
  9.2 0.0 collective-permute-done.mate
  9.2 3.4 %first.1 = (f32[4,128,128]{2,1,0:T(8,128)S(1)}, f32[128,128]{1,0:T(8,128)S(1)}) custom-call(f32[512,128]{1,0:T(8,128)S(1)} %convert_element_type.3.own, bf16[512,128]{1,0:T(8,128)(2,1)S(1)} %collective-permute-done.mate, bf16[256,128]{1,0:T(8,128)(2,1)S(1)} %collective-permute-done.1.far, bf16[256,128]{1,0:T(8,128)(2,1)S(1)} %collective-permute-done.2.far_mate), custom_call_target="tpu_custom_call" | custom-call | flops 300000000 | bytes 1000000 | tf_op jit(solution)/shard_map/first/pallas_call | solution.py:297
  12.6 0.0 collective-permute-done.4
  12.6 0.1 compare_select_fusion.refs_2_
  12.8 2.4 %collective-permute-start.5 = (bf16[128,512]{1,0:T(8,128)(2,1)S(1)}, bf16[128,512]{1,0:T(8,128)(2,1)S(1)}, u32[]{:S(2)}, u32[]{:S(2)}) collective-permute-start(bf16[128,512]{1,0:T(8,128)(2,1)S(1)} %compare_select_fusion.refs_2_), channel_id=1, source_target_pairs={{16,0},{20,4},{24,8},{28,12},{0,16},{4,20},{8,24},{12,28},{17,1},{... | collective-permute-start | bytes 393224 | tf_op jit(solution)/shard_map/ppermute | solution.py:339
  15.1 3.9 %collective-permute-start.6 = (bf16[128,512]{1,0:T(8,128)(2,1)S(1)}, bf16[128,512]{1,0:T(8,128)(2,1)S(1)}, u32[]{:S(2)}, u32[]{:S(2)}) collective-permute-start(bf16[128,512]{1,0:T(8,128)(2,1)S(1)} %compare_select_fusion.refs_2_), channel_id=1, source_target_pairs={{0,0},{4,1},{8,2},{12,3},{16,4},{20,5},{24,6},{28,7},{1,8},{5,9},{... | collective-permute-start | bytes 393224 | tf_op jit(solution)/shard_map/ppermute | solution.py:327
  19.0 0.0 copy-start
  19.0 12.1 %rest.1 = (f32[512,128]{1,0:T(8,128)}, bf16[512,512]{1,0:T(8,128)(2,1)S(1)}, bf16[512,512]{1,0:T(8,128)(2,1)S(1)}) custom-call(f32[512,128]{1,0:T(8,128)S(1)} %convert_element_type.3.own, bf16[512,128]{1,0:T(8,128)(2,1)S(1)} %collective-permute-done.mate, bf16[256,128]{1,0:T(8,128)(2,1)S(1)} %collective-permute-done.1.far, ...), custom_call_target="tpu_custom_call" | custom-call | flops 1000000000 | bytes 2000000 | tf_op jit(solution)/shard_map/rest/pallas_call | solution.py:346
  31.1 0.0 collective-permute-done.5.refs_3_
  31.1 0.0 collective-permute-done.6.refs_4_
  31.1 1.4 %solve.1 = (bf16[1,32,512]{2,1,0:T(8,128)(2,1)}, bf16[256,128]{1,0:T(8,128)(2,1)}) custom-call(bf16[512,512]{1,0:T(8,128)(2,1)S(1)} %get-tuple-element.16.refs_0_, bf16[512,512]{1,0:T(8,128)(2,1)S(1)} %get-tuple-element.17.refs_1_, bf16[128,512]{1,0:T(8,128)(2,1)S(1)} %compare_select_fusion.refs_2_, bf16[128,512]{1,0:T(8,128)(2,1)S(1)} %collective-permute-done.5.refs_3_, ...), custom_call_target="tpu_custom_call" | custom-call | flops 400000000 | bytes 2000000 | tf_op jit(solution)/shard_map/solve/pallas_call | solution.py:365
  (11 shorter events, 0.1 us)
Async XLA Ops:
  0.6 8.6 %collective-permute-start = (bf16[512,128]{1,0:T(8,128)(2,1)}, bf16[512,128]{1,0:T(8,128)(2,1)S(1)}, u32[]{:S(2)}, u32[]{:S(2)}) collective-permute-start(bf16[512,128]{1,0:T(8,128)(2,1)} %param.4), channel_id=1, source_target_pairs={{1,0},{0,1},{3,2},{2,3},{5,4},{4,5},{7,6},{6,7},{9,8},{8,9},{11,10... | collective-permute-start | bytes 393224 | tf_op jit(solution)/shard_map/ppermute | solution.py:294
  0.8 3.6 %copy-start.2 = (bf16[1,32,512]{2,1,0:T(8,128)(2,1)S(1)}, bf16[1,32,512]{2,1,0:T(8,128)(2,1)}, u32[]{:S(2)}) copy-start(bf16[1,32,512]{2,1,0:T(8,128)(2,1)} %param.5) | copy-start | bytes 98308
  0.8 8.4 %copy-start.1 = (bf16[512,128]{1,0:T(8,128)(2,1)S(1)}, bf16[512,128]{1,0:T(8,128)(2,1)}, u32[]{:S(2)}) copy-start(bf16[512,128]{1,0:T(8,128)(2,1)} %param.4) | copy-start | bytes 393220
  1.7 7.5 %collective-permute-start.1 = (bf16[256,128]{1,0:T(8,128)(2,1)S(1)}, bf16[256,128]{1,0:T(8,128)(2,1)S(1)}, u32[]{:S(2)}, u32[]{:S(2)}) collective-permute-start(bf16[256,128]{1,0:T(8,128)(2,1)S(1)} %constant_dynamic-slice_fusion), channel_id=1, source_target_pairs={{2,0},{3,1},{0,2},{1,3},{6,4},{7,5},{4,6},{5,7},{10,8},{11,9},{8,1... | collective-permute-start | bytes 196616 | tf_op jit(solution)/shard_map/ppermute | solution.py:292
  4.3 4.9 %collective-permute-start.2 = (bf16[256,128]{1,0:T(8,128)(2,1)S(1)}, bf16[256,128]{1,0:T(8,128)(2,1)S(1)}, u32[]{:S(2)}, u32[]{:S(2)}) collective-permute-start(bf16[256,128]{1,0:T(8,128)(2,1)S(1)} %constant_dynamic-slice_fusion), channel_id=1, source_target_pairs={{3,0},{2,1},{1,2},{0,3},{7,4},{6,5},{5,6},{4,7},{11,8},{10,9},{9,1... | collective-permute-start | bytes 196616 | tf_op jit(solution)/shard_map/ppermute | solution.py:293
  4.3 3.3 %collective-permute-start.3 = (bf16[32,512]{1,0:T(8,128)(2,1)S(1)}, bf16[32,512]{1,0:T(8,128)(2,1)S(1)}, u32[]{:S(2)}, u32[]{:S(2)}) collective-permute-start(bf16[32,512]{1,0:T(8,128)(2,1)S(1)} %bitcast.2), channel_id=1, source_target_pairs={{4,0},{0,4},{12,8},{8,12},{20,16},{16,20},{28,24},{24,28},{5,1},{1... | collective-permute-start | bytes 98312 | tf_op jit(solution)/shard_map/ppermute | solution.py:333
  6.1 0.7 %copy-start.3 = (s32[1,2]{1,0:T(1,128)S(1)}, s32[1,2]{1,0:T(1,128)}, u32[]{:S(2)}) copy-start(s32[1,2]{1,0:T(1,128)} %param.6) | copy-start | bytes 28
  7.6 5.0 %collective-permute-start.4 = (bf16[64,512]{1,0:T(8,128)(2,1)S(1)}, bf16[64,512]{1,0:T(8,128)(2,1)S(1)}, u32[]{:S(2)}, u32[]{:S(2)}) collective-permute-start(bf16[64,512]{1,0:T(8,128)(2,1)S(1)} %constant_dynamic-update-slice_fusion), channel_id=1, source_target_pairs={{8,0},{12,4},{0,8},{4,12},{24,16},{28,20},{16,24},{20,28},{9,1},{1... | collective-permute-start | bytes 196616 | tf_op jit(solution)/shard_map/ppermute | solution.py:333
  12.8 18.3 %collective-permute-start.5 = (bf16[128,512]{1,0:T(8,128)(2,1)S(1)}, bf16[128,512]{1,0:T(8,128)(2,1)S(1)}, u32[]{:S(2)}, u32[]{:S(2)}) collective-permute-start(bf16[128,512]{1,0:T(8,128)(2,1)S(1)} %compare_select_fusion.refs_2_), channel_id=1, source_target_pairs={{16,0},{20,4},{24,8},{28,12},{0,16},{4,20},{8,24},{12,28},{17,1},{... | collective-permute-start | bytes 393224 | tf_op jit(solution)/shard_map/ppermute | solution.py:339
  15.1 16.0 %collective-permute-start.6 = (bf16[128,512]{1,0:T(8,128)(2,1)S(1)}, bf16[128,512]{1,0:T(8,128)(2,1)S(1)}, u32[]{:S(2)}, u32[]{:S(2)}) collective-permute-start(bf16[128,512]{1,0:T(8,128)(2,1)S(1)} %compare_select_fusion.refs_2_), channel_id=1, source_target_pairs={{0,0},{4,1},{8,2},{12,3},{16,4},{20,5},{24,6},{28,7},{1,8},{5,9},{... | collective-permute-start | bytes 393224 | tf_op jit(solution)/shard_map/ppermute | solution.py:327
  19.0 12.1 %copy-start = (bf16[256,128]{1,0:T(8,128)(2,1)S(1)}, bf16[256,128]{1,0:T(8,128)(2,1)}, u32[]{:S(2)}) copy-start(bf16[256,128]{1,0:T(8,128)(2,1)} %refs_5_.1) | copy-start | bytes 196612
